TPU v7x, 32 devices: a whole 2x2x4 slice. The times are simulated.
32 devices in a mesh: seq: 8 (over y, x, core), tensor: 4 (over z).
Axes of the slice: x: 2, y: 2, z: 4, core: 2. Of those that a mesh axis runs over, the one named last changes fastest.
Arguments:
- tokens: bfloat16 [4096, 4096], P('seq', 'tensor'), may hold values from -6 to 6
- norm_gain: float32 [4096], replicated, may hold values from 0.1 to 1.9
- w_query: bfloat16 [4096, 4096], P('seq', 'tensor'), may hold values from -0.09375 to 0.09375
- w_key: bfloat16 [4096, 4096], P('seq', 'tensor'), may hold values from -0.09375 to 0.09375
- w_value: bfloat16 [4096, 4096], P('seq', 'tensor'), may hold values from -0.09375 to 0.09375
- out_gain: float32 [4096], P('tensor'), may hold values from 0.1 to 1.9
- carried: float32 [32, 128, 128], P('tensor'), may hold values from -384 to 384
Outputs:
- attended: bfloat16 [4096, 4096], P('seq', 'tensor')
- final_state: float32 [32, 128, 128], P('tensor')
All inputs are finite; a program needn't handle non-finite values.
Results may differ from a plain program's by a relative error of at most 0.009.
Values may be sent and summed in bfloat16 or wider, within the bound.
A program may use at most 64 MiB of HBM per device.

v0:
```python
import jax
import jax.numpy as jnp
from jax import lax
from jax.sharding import PartitionSpec as P

BLOCK = 512


def add_rows(normed, pieces):
    return tuple((jnp.dot(normed, piece, preferred_element_type=jnp.float32) for piece in pieces))


def shards(tokens, norm_gain, w_query, w_key, w_value, out_gain, carried):
    whole = lax.all_gather(tokens, "tensor", axis=1, tiled=True)
    xf = whole.astype(jnp.float32)
    normed = (xf * lax.rsqrt(jnp.mean(xf * xf, axis=1, keepdims=True) + 1e-05) * norm_gain).astype(
        jnp.bfloat16
    )
    rows = normed.shape[0]
    width = w_query.shape[1]
    size = carried.shape[1]
    heads = width // size
    qsum, ksum, vsum = add_rows(
        normed,
        (
            lax.all_gather(w_query, "seq", axis=0, tiled=True),
            lax.all_gather(w_key, "seq", axis=0, tiled=True),
            lax.all_gather(w_value, "seq", axis=0, tiled=True),
        ),
    )
    blocks = rows // BLOCK
    query = qsum.astype(jnp.bfloat16).reshape(blocks, BLOCK, heads, size)
    key = ksum.astype(jnp.bfloat16).reshape(blocks, BLOCK, heads, size)
    value = vsum.astype(jnp.bfloat16).reshape(blocks, BLOCK, heads, size)
    block_state = jnp.einsum("nthd,nthe->nhde", key, value, preferred_element_type=jnp.float32)
    local_total = jnp.sum(block_state, axis=0)
    zero_state = jnp.zeros_like(local_total)
    mine = lax.axis_index("seq")
    piece = lax.all_gather(
        local_total[None].astype(jnp.bfloat16), "seq", axis=0, tiled=True
    ).astype(jnp.float32)
    where = jnp.arange(piece.shape[0], dtype=jnp.int32)
    keep = (where < mine).astype(jnp.float32)
    before = zero_state + jnp.sum(keep[:, None, None, None] * piece, axis=0)
    total = zero_state + jnp.sum(piece, axis=0)
    start_state = carried + before
    running = jnp.cumsum(block_state, axis=0) - block_state
    priors = start_state[None] + running
    inter = jnp.einsum(
        "nthd,nhde->nthe", query.astype(jnp.float32), priors, precision=lax.Precision.HIGHEST
    )
    causal = jnp.tril(jnp.ones((BLOCK, BLOCK), jnp.float32))
    scores = jnp.einsum("nthd,nshd->nhts", query, key, preferred_element_type=jnp.float32)
    weights = (scores * causal).astype(jnp.bfloat16)
    intra = jnp.einsum("nhts,nshe->nthe", weights, value, preferred_element_type=jnp.float32)
    raw = inter + intra
    normal = (
        raw
        * lax.rsqrt(jnp.mean(raw * raw, axis=3, keepdims=True) + 1e-06)
        * out_gain.reshape(heads, size)
    )
    attended = normal.astype(jnp.bfloat16).reshape(rows, width)
    return (attended, carried + total)


def solution(mesh):
    return jax.shard_map(
        shards,
        mesh=mesh,
        in_specs=(
            P("seq", "tensor"),
            P(),
            P("seq", "tensor"),
            P("seq", "tensor"),
            P("seq", "tensor"),
            P("tensor"),
            P("tensor", None, None),
        ),
        out_specs=(P("seq", "tensor"), P("tensor", None, None)),
        check_vma=False,
    )
```

profile of v0, /device:TPU:0, one launch (start us, length us, event | category | flops | bytes accessed | tf_op | source)
XLA Modules:
  0.0 313.7 jit_solution(12535060636270951902)
XLA Ops:
  7.2 0.7 all-gather.7.cloned.1.call-update
  8.0 0.7 all-gather.9.cloned.1.call-update
  8.7 0.7 all-gather.11.cloned.1.call-update
  9.4 0.5 all-gather.13.cloned.1.call-update
  10.0 0.0 all-gather.15.cloned.1.call-start
  10.0 83.1 %all-gather.7.cloned.1.call-done = bf16[512,4096]{1,0:T(8,128)(2,1)} async-done(((bf16[512,1024]{1,0:T(8,128)(2,1)}), bf16[512,4096]{1,0:T(8,128)(2,1)}) %all-gather.7.cloned.1.call-update) | async-done | bytes 4194320 | tf_op jit(solution)/shard_map/all_gather | solution.py:14
  93.1 3.1 fusion
  96.2 51.7 %all-gather.9.cloned.1.call-done = bf16[4096,1024]{1,0:T(8,128)(2,1)} async-done(((bf16[512,1024]{1,0:T(8,128)(2,1)}), bf16[4096,1024]{1,0:T(8,128)(2,1)}) %all-gather.9.cloned.1.call-update) | async-done | bytes 8388624 | tf_op jit(solution)/shard_map/all_gather | solution.py:27
  147.9 9.2 %convolution_convert_fusion.2 = bf16[512,1024]{1,0:T(8,128)(2,1)S(1)} fusion(bf16[4096,1024]{1,0:T(8,128)(2,1)} %all-gather.9.cloned.1.call-done, bf16[512,4096]{1,0:T(8,128)(2,1)} %all-gather.7.cloned.1.call-done, f32[4096]{0:T(1024)S(1)} %copy-done.3, f32[512]{0:T(512)S(1)} %add_rsqrt_fusion.1), kind=kOutput, calls=%fused_computation.20 | convolution fusion | flops 4303880192 | bytes 13649920 | tf_op jit(solution)/shard_map/dot_general | solution.py:10
  157.1 0.7 copy.22
  157.9 46.4 %all-gather.11.cloned.1.call-done = bf16[4096,1024]{1,0:T(8,128)(2,1)} async-done(((bf16[512,1024]{1,0:T(8,128)(2,1)}), bf16[4096,1024]{1,0:T(8,128)(2,1)}) %all-gather.11.cloned.1.call-update) | async-done | bytes 8388624 | tf_op jit(solution)/shard_map/all_gather | solution.py:28
  204.2 9.2 %convolution_convert_fusion.1 = bf16[512,1024]{1,0:T(8,128)(2,1)S(1)} fusion(bf16[4096,1024]{1,0:T(8,128)(2,1)} %all-gather.11.cloned.1.call-done, bf16[512,4096]{1,0:T(8,128)(2,1)} %all-gather.7.cloned.1.call-done, f32[4096]{0:T(1024)S(1)} %copy-done.3, f32[512]{0:T(512)S(1)} %add_rsqrt_fusion.1), kind=kOutput, calls=%fused_computation.19 | convolution fusion | flops 4303880192 | bytes 13649920 | tf_op jit(solution)/shard_map/dot_general | solution.py:10
  213.4 0.5 copy.23
  214.0 1.3 fusion.27
  215.3 0.1 fusion.17
  215.5 44.9 %all-gather.13.cloned.1.call-done = bf16[4096,1024]{1,0:T(8,128)(2,1)} async-done(((bf16[512,1024]{1,0:T(8,128)(2,1)}), bf16[4096,1024]{1,0:T(8,128)(2,1)}) %all-gather.13.cloned.1.call-update) | async-done | bytes 8388624 | tf_op jit(solution)/shard_map/all_gather | solution.py:26
  260.4 10.2 %fusion.12 = bf16[64,8,8,128]{3,2,1,0:T(8,128)(2,1)} fusion(bf16[4096,1024]{1,0:T(8,128)(2,1)} %all-gather.13.cloned.1.call-done, bf16[512,4096]{1,0:T(8,128)(2,1)} %all-gather.7.cloned.1.call-done, f32[4096]{0:T(1024)S(1)} %copy-done.3, f32[512]{0:T(512)S(1)} %add_rsqrt_fusion.1), kind=kOutput, calls=%fused_computation.21 | convolution fusion | flops 4303880192 | bytes 13649920 | tf_op jit(solution)/shard_map/dot_general | solution.py:10
  270.6 19.5 %all-gather.15.cloned.1.call-done = bf16[64,128,128]{2,1,0:T(8,128)(2,1)} async-done(((bf16[8,128,128]{2,1,0:T(8,128)(2,1)}), bf16[64,128,128]{2,1,0:T(8,128)(2,1)}) %all-gather.15.cloned.1.call-update) | async-done | bytes 2097168 | tf_op jit(solution)/shard_map/all_gather | solution.py:39
  290.1 3.2 %convert_reduce_fusion = (f32[8,128,128]{2,1,0:T(8,128)}, f32[8,128,128]{2,1,0:T(8,128)S(1)}) fusion(bf16[8,8,128,128]{3,2,1,0:T(8,128)(2,1)} %bitcast.39, f32[8]{0:T(128)S(1)} %compare_convert_fusion), kind=kLoop, calls=%fused_computation.6 | loop fusion | flops 3932160 | bytes 3145760 | tf_op jit(solution)/shard_map/reduce_sum | solution.py:45
  293.3 3.9 %fusion.15 = f32[8,128,512]{2,1,0:T(8,128)} fusion(bf16[64,8,8,128]{3,2,1,0:T(8,128)(2,1)} %fusion.12, f32[8,128,128]{2,1,0:T(8,128)} %get-tuple-element.9, f32[8,128,128]{2,1,0:T(8,128)} %param.13, f32[8,128,128]{2,1,0:T(8,128)S(1)} %get-tuple-element.7), kind=kOutput, calls=%fused_computation.23 | convolution fusion | flops 805699584 | bytes 4718592 | tf_op jit(solution)/shard_map/nthd,nhde->nthe/dot_general | solution.py:49
  297.2 5.8 %fusion.8 = (f32[512,8]{0,1:T(8,128)S(1)}, f32[8,128,512]{2,1,0:T(8,128)}) fusion(f32[8,128,512]{2,1,0:T(8,128)} %fusion.15, bf16[512,8,128]{0,2,1:T(8,128)(2,1)S(1)} %bitcast.37, f32[512,512]{1,0:T(8,128)S(1)} %fusion.17, bf16[512,8,128]{0,2,1:T(8,128)(2,1)S(1)} %bitcast.35, bf16[64,8,8,128]{3,2,1,0:T(8,128)(2,1)} %fusion.12), kind=kOutput, calls=%fused_computation.14 | convolution fusion | flops 1079504896 | bytes 8404992 | tf_op jit(solution)/shard_map/nhts,nshe->nthe/dot_general | solution.py:55
  303.0 2.0 fusion.10
  305.0 1.3 copy.20
  306.3 0.8 add.52
  (16 shorter events, 0.2 us)
Async XLA Ops:
  7.2 140.8 %copy-start.3 = (f32[4096]{0:T(1024)S(1)}, f32[4096]{0:T(1024)}, u32[]{:S(2)}) copy-start(f32[4096]{0:T(1024)} %param.8) | copy-start | bytes 49156
  7.2 85.9 %all-gather.7.cloned.1.call-start = ((), (), s32[]{:S(2)}) async-start(), calls=%async_computation | async-start | bytes 5242880 | tf_op jit(solution)/shard_map/all_gather | solution.py:14
  7.9 140.0 %all-gather.9.cloned.1.call-start = ((), (), s32[]{:S(2)}) async-start(), calls=%async_computation.1 | async-start | bytes 9437184 | tf_op jit(solution)/shard_map/all_gather | solution.py:27
  8.7 195.6 %all-gather.11.cloned.1.call-start = ((), (), s32[]{:S(2)}) async-start(), calls=%async_computation.2 | async-start | bytes 9437184 | tf_op jit(solution)/shard_map/all_gather | solution.py:28
  9.4 251.0 %all-gather.13.cloned.1.call-start = ((), (), s32[]{:S(2)}) async-start(), calls=%async_computation.3 | async-start | bytes 9437184 | tf_op jit(solution)/shard_map/all_gather | solution.py:26
  10.0 280.1 %all-gather.15.cloned.1.call-start = ((), (), s32[]{:S(2)}) async-start(), calls=%async_computation.4 | async-start | bytes 2359296 | tf_op jit(solution)/shard_map/all_gather | solution.py:39
  297.2 5.8 %copy-start.2 = (f32[1024]{0:T(1024)S(1)}, f32[1024]{0:T(1024)}, u32[]{:S(2)}) copy-start(f32[1024]{0:T(1024)} %param.12) | copy-start | bytes 12292
  303.0 3.3 %copy-start = (f32[8,128,128]{2,1,0:T(8,128)S(1)}, f32[8,128,128]{2,1,0:T(8,128)}, u32[]{:S(2)}) copy-start(f32[8,128,128]{2,1,0:T(8,128)} %param.13) | copy-start | bytes 1572868
  303.0 3.3 %copy-start.1 = (f32[8,128,128]{2,1,0:T(8,128)S(1)}, f32[8,128,128]{2,1,0:T(8,128)}, u32[]{:S(2)}) copy-start(f32[8,128,128]{2,1,0:T(8,128)} %get-tuple-element.6) | copy-start | bytes 1572868
Sparse Core Ops, SparseCore 0:
  9.6 83.4 all-gather.6
  95.0 52.9 all-gather.8
  149.8 54.3 all-gather.10
  206.0 54.3 all-gather.12
  262.1 27.8 all-gather.14
where the time goes:
time: 314 us
  waiting for transfers between devices  248 us (79%)
  matrix products  39.6 us (13%)
  between operations  13.9 us (4%)
  other arithmetic  9.22 us (3%)
    all_gather x1, waiting for transfers between devices, shards(): whole = lax.all_gather(tokens, 'tensor', axis=1, tiled=True)  83.1 us
    all_gather x1, waiting for transfers between devices, shards(): lax.all_gather(w_key, 'seq', axis=0, tiled=True)  51.7 us
    all_gather x1, waiting for transfers between devices, shards(): lax.all_gather(w_value, 'seq', axis=0, tiled=True)  46.4 us
    all_gather x1, waiting for transfers between devices, shards(): lax.all_gather(w_query, 'seq', axis=0, tiled=True)  44.9 us
    dot_general x3, matrix products, add_rows(): jnp.dot(normed, piece, preferred_element_type=jnp.float32)  28.6 us
    all_gather x1, waiting for transfers between devices, shards(): lax.all_gather(local_total[None].astype(jnp.bfloat16), 'seq', axis=0, til...  19.5 us
  transfers between devices with their start and end apart: 5, of which 5 were waited for; matrix products, arithmetic and copies ran while one was open for 11% of the time, Pallas kernels for 0%

commit v1 on v0

--- a/solution.py
+++ b/solution.py
@@ -1,9 +1,17 @@
+import functools
+
 import jax
 import jax.numpy as jnp
 from jax import lax
+from jax.experimental import pallas as pl
+from jax.experimental.pallas import tpu as pltpu
 from jax.sharding import PartitionSpec as P
 
 BLOCK = 512
+MESH = pl.DeviceIdType.MESH
+GROUP = 256
+PARTS = 4
+AHEAD = 3
 
 
 def add_rows(normed, pieces):
@@ -63,9 +71,446 @@
     return (attended, carried + total)
 
 
+def dot(a, b, dims=((1,), (0,))):
+    return lax.dot_general(a, b, (dims, ((), ())), preferred_element_type=jnp.float32)
+
+
+def kernel(
+    depth_z,
+    tokens,
+    norm_gain,
+    w_query,
+    w_key,
+    w_value,
+    out_gain,
+    carried,
+    attended,
+    final,
+    tok,
+    normed,
+    buf,
+    proj,
+    state_out,
+    state_sib,
+    sum_out,
+    sum_in,
+    prior,
+    local_sem,
+    w_send,
+    w_recv,
+    t_send,
+    t_recv,
+    s_send,
+    s_recv,
+):
+    rows, shard = tokens.shape
+    depth = w_query.shape[0]
+    groups = w_query.shape[1] // GROUP
+    size = carried.shape[1]
+    heads = carried.shape[0]
+    per = GROUP // size
+    half = heads // 2
+    early = 2 * groups
+    chunks = 3 * groups
+    part = rows // PARTS
+    hops = depth_z - 1
+
+    seq = lax.axis_index("seq")
+    z = lax.axis_index("tensor")
+    c = seq % 2
+    x = (seq // 2) % 2
+    y = seq // 4
+    sib = y * 4 + x * 2 + (1 - c)
+    xn = y * 4 + (1 - x) * 2 + c
+    yn = (1 - y) * 4 + x * 2 + c
+    diag = (1 - y) * 4 + (1 - x) * 2 + c
+    x_sib = y * 4 + (1 - x) * 2 + (1 - c)
+    y_sib = (1 - y) * 4 + x * 2 + (1 - c)
+    diag_sib = (1 - y) * 4 + (1 - x) * 2 + (1 - c)
+
+    tok_copy = pltpu.make_async_copy(tokens, tok.at[z], local_sem.at[chunks])
+    tok_copy.start()
+    own_copies = []
+    for ch in range(chunks):
+        if ch < early:
+            ref, g = (w_key, w_value)[ch % 2], ch // 2
+        else:
+            ref, g = w_query, ch - early
+        copy = pltpu.make_async_copy(
+            ref.at[:, pl.ds(g * GROUP, GROUP)],
+            buf.at[ch, pl.ds(pl.multiple_of(seq * depth, depth), depth), :],
+            local_sem.at[ch],
+        )
+        copy.start()
+        own_copies.append(copy)
+
+    barrier = pltpu.get_barrier_semaphore()
+    for other in (sib, xn, yn):
+        pl.semaphore_signal(barrier, inc=1, device_id=(other, z), device_id_type=MESH)
+
+    @pl.when(z > 0)
+    def _():
+        pl.semaphore_signal(barrier, inc=1, device_id=(seq, z - 1), device_id_type=MESH)
+
+    @pl.when(z < depth_z - 1)
+    def _():
+        pl.semaphore_signal(barrier, inc=1, device_id=(seq, z + 1), device_id_type=MESH)
+
+    pl.semaphore_wait(barrier, 3 + jnp.minimum(z, 1) + jnp.minimum(depth_z - 1 - z, 1))
+
+    def piece(ch, kind, owner, target, first=0, count=None):
+        count = depth if count is None else count
+        at = buf.at[ch, pl.ds(pl.multiple_of(owner * depth + first, count), count), :]
+        return pltpu.make_async_remote_copy(
+            src_ref=at,
+            dst_ref=at,
+            send_sem=w_send.at[ch, kind],
+            recv_sem=w_recv.at[ch, kind],
+            device_id=(target, z),
+            device_id_type=MESH,
+        )
+
+    mid = depth // 2
+
+    def outgoing(ch, kind):
+        places = (
+            (seq, xn),
+            (seq, yn),
+            (seq, sib),
+            (xn, yn, 0, mid),
+            (yn, xn, mid, mid),
+            (xn, sib),
+            (yn, sib),
+            (diag, sib),
+        )
+        return piece(ch, kind, *places[kind])
+
+    def incoming(ch, kind):
+        places = (
+            (xn, xn),
+            (yn, yn),
+            (sib, sib),
+            (diag, yn, 0, mid),
+            (diag, xn, mid, mid),
+            (x_sib, sib),
+            (y_sib, sib),
+            (diag_sib, sib),
+        )
+        return piece(ch, kind, *places[kind])
+
+    def send_own(ch):
+        for kind in (0, 1, 2):
+            outgoing(ch, kind).start()
+
+    def pass_near(ch):
+        incoming(ch, 0).wait_recv()
+        outgoing(ch, 3).start()
+        outgoing(ch, 5).start()
+        incoming(ch, 1).wait_recv()
+        outgoing(ch, 4).start()
+        outgoing(ch, 6).start()
+
+    def pass_far(ch):
+        incoming(ch, 3).wait_recv()
+        incoming(ch, 4).wait_recv()
+        outgoing(ch, 7).start()
+
+    def complete(ch):
+        for kind in (2, 5, 6, 7):
+            incoming(ch, kind).wait_recv()
+
+    def token_copy(way, hop, p, owner):
+        at = tok.at[owner, pl.ds(pl.multiple_of(p * part, part), part), :]
+        target = z + 1 if way == 0 else z - 1
+        return pltpu.make_async_remote_copy(
+            src_ref=at,
+            dst_ref=at,
+            send_sem=t_send.at[way, hop, p],
+            recv_sem=t_recv.at[way, hop, p],
+            device_id=(seq, target),
+            device_id_type=MESH,
+        )
+
+    def token_step(t):
+        hop, p = t // PARTS, t % PARTS
+
+        @pl.when(z - 1 - hop >= 0)
+        def _():
+            token_copy(0, hop, p, z - 1 - hop).wait_recv()
+
+            @pl.when(z < depth_z - 1)
+            def _():
+                token_copy(0, hop + 1, p, z - 1 - hop).start()
+
+        @pl.when(z + 1 + hop < depth_z)
+        def _():
+            token_copy(1, hop, p, z + 1 + hop).wait_recv()
+
+            @pl.when(z > 0)
+            def _():
+                token_copy(1, hop + 1, p, z + 1 + hop).start()
+
+    own_copies[0].wait()
+    send_own(0)
+    tok_copy.wait()
+
+    @pl.loop(0, PARTS)
+    def _(p):
+        @pl.when(z < depth_z - 1)
+        def _():
+            token_copy(0, 0, p, z).start()
+
+        @pl.when(z > 0)
+        def _():
+            token_copy(1, 0, p, z).start()
+
+    for ch in range(1, chunks):
+        own_copies[ch].wait()
+    for ch in range(1, AHEAD):
+        send_own(ch)
+
+    def normalise():
+        step = 32
+
+        @pl.loop(0, rows // step)
+        def _(r):
+            at = pl.ds(pl.multiple_of(r * step, step), step)
+            squares = jnp.zeros((step, 1), jnp.float32)
+            for k in range(depth_z):
+                v = tok[k, at, :].astype(jnp.float32)
+                squares = squares + jnp.sum(v * v, axis=1, keepdims=True)
+            scale = lax.rsqrt(squares / (depth_z * shard) + 1e-05)
+            for k in range(depth_z):
+                v = tok[k, at, :].astype(jnp.float32)
+                gain = norm_gain[:, k * shard : (k + 1) * shard]
+                normed[at, k * shard : (k + 1) * shard] = (v * scale * gain).astype(jnp.bfloat16)
+
+    def project(ch):
+        complete(ch)
+        proj[ch] = dot(normed[...], buf[ch]).astype(jnp.bfloat16)
+
+    def early_chunk(ch):
+        project(ch)
+
+        @pl.when(ch % 2 == 1)
+        def _():
+            both = dot(proj[ch - 1], proj[ch], ((0,), (0,)))
+            for e in range(per):
+                st = both[e * size : (e + 1) * size, e * size : (e + 1) * size]
+                state_out[ch // 2 * per + e] = st.astype(jnp.bfloat16)
+
+    mine = pl.ds(c * half, half)
+    theirs = pl.ds((1 - c) * half, half)
+
+    def state_copy(k, source, target_ref, target):
+        return pltpu.make_async_remote_copy(
+            src_ref=source,
+            dst_ref=target_ref,
+            send_sem=s_send.at[k],
+            recv_sem=s_recv.at[k],
+            device_id=(target, z),
+            device_id_type=MESH,
+        )
+
+    to_sib = state_copy(0, state_out, state_sib, sib)
+    to_x = state_copy(1, sum_out.at[0], sum_in.at[0, mine], xn)
+    x_to_sib = state_copy(2, sum_in.at[0, mine], sum_in.at[0, mine], sib)
+    to_y = state_copy(3, sum_out.at[1], sum_in.at[1, mine], yn)
+    y_to_sib = state_copy(4, sum_in.at[1, mine], sum_in.at[1, mine], sib)
+    x_from_sib = state_copy(2, sum_in.at[0, theirs], sum_in.at[0, theirs], sib)
+    y_from_sib = state_copy(4, sum_in.at[1, theirs], sum_in.at[1, theirs], sib)
+
+    def wide(v):
+        return v.astype(jnp.float32)
+
+    def state_one():
+        to_sib.start()
+
+    def state_two():
+        to_sib.wait_recv()
+        sum_out[0] = (wide(state_out[mine]) + wide(state_sib[mine])).astype(jnp.bfloat16)
+        to_x.start()
+
+    def state_three():
+        to_x.wait_recv()
+        x_to_sib.start()
+        sum_out[1] = (wide(sum_out[0]) + wide(sum_in[0, mine])).astype(jnp.bfloat16)
+        to_y.start()
+
+    def state_four():
+        to_y.wait_recv()
+        y_to_sib.start()
+
+    def state_five():
+        x_from_sib.wait_recv()
+        y_from_sib.wait_recv()
+        on_c = c.astype(jnp.float32)
+        on_x = x.astype(jnp.float32)
+        on_y = y.astype(jnp.float32)
+        for h in range(heads):
+            near = wide(state_sib[h])
+            chip = (wide(state_out[h]) + near).astype(jnp.bfloat16)
+            beside = wide(sum_in[0, h])
+            row = (wide(chip) + beside).astype(jnp.bfloat16)
+            far = wide(sum_in[1, h])
+            start = carried[h]
+            before = near * on_c + beside * on_x + far * on_y
+            prior[h] = (start + before).astype(jnp.bfloat16)
+            final[h] = start + (wide(row) + far)
+
+    top = rows // 2
+
+    def attend(g):
+        at = lax.broadcasted_iota(jnp.int32, (top, top), 0)
+        of = lax.broadcasted_iota(jnp.int32, (top, top), 1)
+        causal = of <= at
+
+        def masked(s):
+            return jnp.where(causal, s, 0.0).astype(jnp.bfloat16)
+
+        for e in range(per):
+            cols = slice(e * size, (e + 1) * size)
+            h = g * per + e
+            start = prior[h]
+            q0, q1 = proj[early + g, :top, cols], proj[early + g, top:, cols]
+            k0, k1 = proj[2 * g, :top, cols], proj[2 * g, top:, cols]
+            v0, v1 = proj[2 * g + 1, :top, cols], proj[2 * g + 1, top:, cols]
+            across = ((1,), (1,))
+            raw0 = dot(q0, start) + dot(masked(dot(q0, k0, across)), v0)
+            raw1 = (
+                dot(q1, start)
+                + dot(dot(q1, k0, across).astype(jnp.bfloat16), v0)
+                + dot(masked(dot(q1, k1, across)), v1)
+            )
+            gain = out_gain[:, h * size : (h + 1) * size]
+            for first, raw in ((0, raw0), (top, raw1)):
+                scale = lax.rsqrt(jnp.mean(raw * raw, axis=1, keepdims=True) + 1e-06)
+                attended[first : first + top, h * size : (h + 1) * size] = (
+                    raw * scale * gain
+                ).astype(jnp.bfloat16)
+
+    steps = hops * PARTS
+
+    @pl.loop(0, chunks)
+    def _(i):
+        @pl.when(i + AHEAD < chunks)
+        def _():
+            send_own(i + AHEAD)
+
+        pass_near(i)
+
+        @pl.when(i > 0)
+        def _():
+            pass_far(i - 1)
+
+        @pl.when(i < early)
+        def _():
+            @pl.loop(i * steps // early, (i + 1) * steps // early)
+            def _(t):
+                token_step(t)
+
+        @pl.when(i == early - 1)
+        def _():
+            normalise()
+
+        @pl.when((i >= early) & (i < chunks - 1))
+        def _():
+            k = i - early
+            span = groups - 1
+
+            @pl.loop(k * early // span, (k + 1) * early // span)
+            def _(ch):
+                early_chunk(ch)
+
+    state_one()
+    project(early)
+    state_two()
+    project(early + 1)
+    state_three()
+    state_four()
+    state_five()
+    for g in range(groups):
+        if g == groups - 1:
+            pass_far(chunks - 1)
+        if g >= 2:
+            project(early + g)
+        attend(g)
+
+    @pl.loop(0, chunks)
+    def _(ch):
+        for kind in range(8):
+            outgoing(ch, kind).wait_send()
+
+    @pl.loop(0, steps)
+    def _(t):
+        hop, p = t // PARTS, t % PARTS
+
+        @pl.when((z < depth_z - 1) & (z - hop >= 0))
+        def _():
+            token_copy(0, hop, p, z - hop).wait_send()
+
+        @pl.when((z > 0) & (z + hop < depth_z))
+        def _():
+            token_copy(1, hop, p, z + hop).wait_send()
+
+    for copy in (to_sib, to_x, x_to_sib, to_y, y_to_sib):
+        copy.wait_send()
+
+
+def fused(depth_z, tokens, norm_gain, w_query, w_key, w_value, out_gain, carried):
+    rows, shard = tokens.shape
+    depth, width = w_query.shape
+    features = norm_gain.shape[0]
+    heads, size = carried.shape[0], carried.shape[1]
+    chunks = 3 * (width // GROUP)
+    any_spec = pl.BlockSpec(memory_space=pl.ANY)
+    vmem_spec = pl.BlockSpec(memory_space=pltpu.VMEM)
+    dma = pltpu.SemaphoreType.DMA
+    return pl.pallas_call(
+        functools.partial(kernel, depth_z),
+        out_shape=(
+            jax.ShapeDtypeStruct((rows, width), jnp.bfloat16),
+            jax.ShapeDtypeStruct(carried.shape, jnp.float32),
+        ),
+        in_specs=[any_spec, vmem_spec, any_spec, any_spec, any_spec, vmem_spec, vmem_spec],
+        out_specs=(vmem_spec, vmem_spec),
+        scratch_shapes=[
+            pltpu.VMEM((depth_z, rows, shard), jnp.bfloat16),
+            pltpu.VMEM((rows, features), jnp.bfloat16),
+            pltpu.VMEM((chunks, features, GROUP), jnp.bfloat16),
+            pltpu.VMEM((chunks, rows, GROUP), jnp.bfloat16),
+            pltpu.VMEM((heads, size, size), jnp.bfloat16),
+            pltpu.VMEM((heads, size, size), jnp.bfloat16),
+            pltpu.VMEM((2, heads // 2, size, size), jnp.bfloat16),
+            pltpu.VMEM((2, heads, size, size), jnp.bfloat16),
+            pltpu.VMEM((heads, size, size), jnp.bfloat16),
+            dma((chunks + 1,)),
+            dma((chunks, 8)),
+            dma((chunks, 8)),
+            dma((2, depth_z, PARTS)),
+            dma((2, depth_z, PARTS)),
+            dma((5,)),
+            dma((5,)),
+        ],
+        compiler_params=pltpu.CompilerParams(
+            collective_id=0, has_side_effects=True, vmem_limit_bytes=56 * 1024 * 1024
+        ),
+        cost_estimate=pl.CostEstimate(
+            flops=6 * rows * features * width, bytes_accessed=8 * depth * width, transcendentals=0
+        ),
+    )(tokens, norm_gain[None], w_query, w_key, w_value, out_gain[None], carried)
+
+
 def solution(mesh):
+    square = mesh.shape["seq"] == 8
+
+    def local(tokens, *rest):
+        if square and tokens.shape[0] == BLOCK:
+            return fused(mesh.shape["tensor"], tokens, *rest)
+        return shards(tokens, *rest)
+
     return jax.shard_map(
-        shards,
+        local,
         mesh=mesh,
         in_specs=(
             P("seq", "tensor"),

time: 314 us -> 140 us (0.45)
  waiting for transfers between devices: 248 us -> 0 us
  Pallas kernels: 0 us -> 136 us
  matrix products: 39.6 us -> 0 us
  between operations: 13.9 us -> 0.65 us
  other arithmetic: 9.22 us -> 0 us
    all_gather x5 -> x0, waiting for transfers between devices: 246 us -> none  [the longest x1 83.1 us: shards(): whole = lax.all_gather(tokens, 'tensor', axis=1, tiled=True)]
    pallas_call x0 -> x1, Pallas kernels: none -> 136 us  [fused(): pl.pallas_call(functools.partial(kernel, depth_z), out_shape=(jax.ShapeDt...]
    dot_general x6 -> x0, matrix products: 39.6 us -> none  [the longest x3 28.6 us: add_rows(): jnp.dot(normed, piece, preferred_element_type=jnp.float32)]
    reduce_sum x2 -> x0, other arithmetic: 6.28 us -> none  [the longest x1 3.2 us: shards(): total = zero_state + jnp.sum(piece, axis=0)]
  transfers between devices with their start and end apart: 5 -> 0, of which waited for: 5 -> 0; matrix products, arithmetic and copies ran while one was open for 11% -> 0% of each run, Pallas kernels for 0% -> 0%
where the time goes in v1:
time: 140 us
  Pallas kernels  136 us (97%)
  local copies, waits for them, and re-layouts  3.12 us (2%)
    pallas_call x1, Pallas kernels, fused(): pl.pallas_call(functools.partial(kernel, depth_z), out_shape=(jax.ShapeDt...  136 us
    unnamed x4, local copies, waits for them, and re-layouts  3.12 us

profile of v1, /device:TPU:0, one launch (start us, length us, event | category | flops | bytes accessed | tf_op | source)
XLA Modules:
  0.0 140.0 jit_solution(11136524749193039526)
XLA Ops:
  0.6 136.3 %shard_map.86 = (bf16[512,1024]{1,0:T(8,128)(2,1)}, f32[8,128,128]{2,1,0:T(8,128)}) custom-call(bf16[512,1024]{1,0:T(8,128)(2,1)} %tokens.1, f32[1,4096]{1,0:T(1,128)} %bitcast.2, bf16[512,1024]{1,0:T(8,128)(2,1)} %w_query.1, bf16[512,1024]{1,0:T(8,128)(2,1)} %w_key.1, bf16[512,1024]{1,0:T(8,128)(2,1)} %w_value.1, f32[1,1024]{1,0:T(1,128)} %bitcast.3, ...), custom_call_target="tpu_custom_call" | custom-call | flops 12884901888 | bytes 4194304 | tf_op jit(solution)/shard_map/pallas_call | solution.py:469
  136.9 0.0 copy-start
  136.9 2.3 %copy.11 = bf16[512,1024]{1,0:T(8,128)(2,1)} copy(bf16[512,1024]{1,0:T(8,128)(2,1)} %get-tuple-element.4) | data formatting | bytes 2097152
  139.2 0.0 copy-done
  139.2 0.8 copy.12
Async XLA Ops:
  136.9 2.3 %copy-start = (f32[8,128,128]{2,1,0:T(8,128)S(1)}, f32[8,128,128]{2,1,0:T(8,128)}, u32[]{:S(2)}) copy-start(f32[8,128,128]{2,1,0:T(8,128)} %get-tuple-element.5) | copy-start | bytes 1572868

commit v2 on v1

--- a/solution.py
+++ b/solution.py
@@ -12,6 +12,8 @@
 GROUP = 256
 PARTS = 4
 AHEAD = 3
+LAG = 2
+LANES = 128
 
 
 def add_rows(normed, pieces):
@@ -87,8 +89,11 @@
     attended,
     final,
     tok,
-    normed,
+    scaled,
+    squares,
+    row_scale,
     buf,
+    acc,
     proj,
     state_out,
     state_sib,
@@ -269,35 +274,49 @@
     for ch in range(1, AHEAD):
         send_own(ch)
 
-    def normalise():
+    def convert(k):
         step = 32
 
         @pl.loop(0, rows // step)
         def _(r):
             at = pl.ds(pl.multiple_of(r * step, step), step)
-            squares = jnp.zeros((step, 1), jnp.float32)
-            for k in range(depth_z):
-                v = tok[k, at, :].astype(jnp.float32)
-                squares = squares + jnp.sum(v * v, axis=1, keepdims=True)
-            scale = lax.rsqrt(squares / (depth_z * shard) + 1e-05)
-            for k in range(depth_z):
-                v = tok[k, at, :].astype(jnp.float32)
-                gain = norm_gain[:, k * shard : (k + 1) * shard]
-                normed[at, k * shard : (k + 1) * shard] = (v * scale * gain).astype(jnp.bfloat16)
-
-    def project(ch):
-        complete(ch)
-        proj[ch] = dot(normed[...], buf[ch]).astype(jnp.bfloat16)
-
-    def early_chunk(ch):
-        project(ch)
-
-        @pl.when(ch % 2 == 1)
+            v = tok[k, at, :].astype(jnp.float32)
+            scaled[k, at, :] = (v * norm_gain[k]).astype(jnp.bfloat16)
+            v = v * v
+            total = squares[at, :]
+            for f in range(shard // LANES):
+                total = total + v[:, f * LANES : (f + 1) * LANES]
+            squares[at, :] = total
+
+    def find_scale():
+        mean = jnp.sum(squares[...], axis=1, keepdims=True) / (depth_z * shard)
+        row_scale[...] = jnp.broadcast_to(lax.rsqrt(mean + 1e-05), (rows, GROUP))
+
+    def accumulate(ch, k):
+        at = pl.ds(pl.multiple_of(k * shard, shard), shard)
+        acc[ch] += dot(scaled[k], buf[ch, at, :])
+
+    def finish(ch):
+        proj[ch] = (acc[ch] * row_scale[...]).astype(jnp.bfloat16)
+
+        @pl.when((ch % 2 == 1) & (ch < early))
         def _():
             both = dot(proj[ch - 1], proj[ch], ((0,), (0,)))
             for e in range(per):
                 st = both[e * size : (e + 1) * size, e * size : (e + 1) * size]
                 state_out[ch // 2 * per + e] = st.astype(jnp.bfloat16)
+
+    def begin(ch, first, last):
+        complete(ch)
+        acc[ch] = jnp.zeros((rows, GROUP), jnp.float32)
+
+        @pl.loop(first, last)
+        def _(k):
+            accumulate(ch, k)
+
+    def project(ch):
+        begin(ch, 0, depth_z)
+        finish(ch)
 
     mine = pl.ds(c * half, half)
     theirs = pl.ds((1 - c) * half, half)
@@ -391,6 +410,9 @@
 
     steps = hops * PARTS
 
+    squares[...] = jnp.zeros_like(squares)
+    convert(z)
+
     @pl.loop(0, chunks)
     def _(i):
         @pl.when(i + AHEAD < chunks)
@@ -399,39 +421,60 @@
 
         pass_near(i)
 
-        @pl.when(i > 0)
-        def _():
-            pass_far(i - 1)
-
-        @pl.when(i < early)
-        def _():
-            @pl.loop(i * steps // early, (i + 1) * steps // early)
-            def _(t):
-                token_step(t)
-
-        @pl.when(i == early - 1)
-        def _():
-            normalise()
-
-        @pl.when((i >= early) & (i < chunks - 1))
-        def _():
-            k = i - early
-            span = groups - 1
-
-            @pl.loop(k * early // span, (k + 1) * early // span)
-            def _(ch):
-                early_chunk(ch)
-
-    state_one()
-    project(early)
+        @pl.when(i >= LAG)
+        def _():
+            pass_far(i - LAG)
+
+        first = jnp.minimum(i * steps // early, steps)
+        last = jnp.minimum((i + 1) * steps // early, steps)
+
+        @pl.loop(first, last)
+        def _(t):
+            token_step(t)
+
+        level = last // PARTS
+        now = i - LAG - 1
+
+        @pl.when(level > first // PARTS)
+        def _():
+            for k in (z - level, z + level):
+
+                @pl.when((k >= 0) & (k < depth_z))
+                def _(k=k):
+                    convert(k)
+
+                    @pl.loop(0, now)
+                    def _(ch):
+                        accumulate(ch, k)
+
+            @pl.when(level == hops)
+            def _():
+                find_scale()
+
+                @pl.loop(0, now)
+                def _(ch):
+                    finish(ch)
+
+        @pl.when(now >= 0)
+        def _():
+            begin(now, jnp.maximum(z - level, 0), jnp.minimum(z + level + 1, depth_z))
+
+            @pl.when(level == hops)
+            def _():
+                finish(now)
+
+        @pl.when(i == early + LAG)
+        def _():
+            state_one()
+
     state_two()
+    pass_far(chunks - 2)
+    state_three()
     project(early + 1)
-    state_three()
     state_four()
+    pass_far(chunks - 1)
     state_five()
     for g in range(groups):
-        if g == groups - 1:
-            pass_far(chunks - 1)
         if g >= 2:
             project(early + g)
         attend(g)
@@ -476,8 +519,11 @@
         out_specs=(vmem_spec, vmem_spec),
         scratch_shapes=[
             pltpu.VMEM((depth_z, rows, shard), jnp.bfloat16),
-            pltpu.VMEM((rows, features), jnp.bfloat16),
+            pltpu.VMEM((depth_z, rows, shard), jnp.bfloat16),
+            pltpu.VMEM((rows, LANES), jnp.float32),
+            pltpu.VMEM((rows, GROUP), jnp.float32),
             pltpu.VMEM((chunks, features, GROUP), jnp.bfloat16),
+            pltpu.VMEM((chunks, rows, GROUP), jnp.float32),
             pltpu.VMEM((chunks, rows, GROUP), jnp.bfloat16),
             pltpu.VMEM((heads, size, size), jnp.bfloat16),
             pltpu.VMEM((heads, size, size), jnp.bfloat16),
@@ -498,7 +544,7 @@
         cost_estimate=pl.CostEstimate(
             flops=6 * rows * features * width, bytes_accessed=8 * depth * width, transcendentals=0
         ),
-    )(tokens, norm_gain[None], w_query, w_key, w_value, out_gain[None], carried)
+    )(tokens, norm_gain.reshape(depth_z, 1, shard), w_query, w_key, w_value, out_gain[None], carried)
 
 
 def solution(mesh):

time: 140 us -> 131 us (0.936)
  Pallas kernels: 136 us -> 126 us
    pallas_call x1, Pallas kernels: 136 us -> 126 us  [fused(): pl.pallas_call(functools.partial(kernel, depth_z), out_shape=(jax.ShapeDt...]
where the time goes in v2:
time: 131 us; the launch traced here: 130 us
  Pallas kernels  126 us (96%)
  local copies, waits for them, and re-layouts  3.12 us (2%)
    pallas_call x1, Pallas kernels, fused(): pl.pallas_call(functools.partial(kernel, depth_z), out_shape=(jax.ShapeDt...  126 us
    unnamed x4, local copies, waits for them, and re-layouts  3.12 us

profile of v2, /device:TPU:0, one launch (start us, length us, event | category | flops | bytes accessed | tf_op | source)
XLA Modules:
  0.0 130.2 jit_solution(4864380762948080437)
XLA Ops:
  0.6 126.5 %shard_map.86 = (bf16[512,1024]{1,0:T(8,128)(2,1)}, f32[8,128,128]{2,1,0:T(8,128)}) custom-call(bf16[512,1024]{1,0:T(8,128)(2,1)} %tokens.1, f32[4,1,1024]{2,1,0:T(1,128)} %bitcast.2, bf16[512,1024]{1,0:T(8,128)(2,1)} %w_query.1, bf16[512,1024]{1,0:T(8,128)(2,1)} %w_key.1, bf16[512,1024]{1,0:T(8,128)(2,1)} %w_value.1, f32[1,1024]{1,0:T(1,128)} %bitcast.3, ...), custom_call_target="tpu_custom_call" | custom-call | flops 12884901888 | bytes 4194304 | tf_op jit(solution)/shard_map/pallas_call | solution.py:512
  127.1 0.0 copy-start
  127.1 2.3 %copy.11 = bf16[512,1024]{1,0:T(8,128)(2,1)} copy(bf16[512,1024]{1,0:T(8,128)(2,1)} %get-tuple-element.4) | data formatting | bytes 2097152
  129.4 0.0 copy-done
  129.5 0.8 copy.12
Async XLA Ops:
  127.1 2.3 %copy-start = (f32[8,128,128]{2,1,0:T(8,128)S(1)}, f32[8,128,128]{2,1,0:T(8,128)}, u32[]{:S(2)}) copy-start(f32[8,128,128]{2,1,0:T(8,128)} %get-tuple-element.5) | copy-start | bytes 1572868

commit v3 on v2

--- a/solution.py
+++ b/solution.py
@@ -11,7 +11,7 @@
 MESH = pl.DeviceIdType.MESH
 GROUP = 256
 PARTS = 4
-AHEAD = 3
+AHEAD = 2
 LAG = 2
 LANES = 128
 
@@ -86,8 +86,8 @@
     w_value,
     out_gain,
     carried,
-    attended,
-    final,
+    attended_out,
+    final_out,
     tok,
     scaled,
     squares,
@@ -107,6 +107,9 @@
     t_recv,
     s_send,
     s_recv,
+    attended,
+    final,
+    o_sem,
 ):
     rows, shard = tokens.shape
     depth = w_query.shape[0]
@@ -338,6 +341,12 @@
     y_to_sib = state_copy(4, sum_in.at[1, mine], sum_in.at[1, mine], sib)
     x_from_sib = state_copy(2, sum_in.at[0, theirs], sum_in.at[0, theirs], sib)
     y_from_sib = state_copy(4, sum_in.at[1, theirs], sum_in.at[1, theirs], sib)
+
+    final_copy = pltpu.make_async_copy(final, final_out, o_sem.at[groups])
+
+    def slab_copy(g):
+        cols = pl.ds(g * GROUP, GROUP)
+        return pltpu.make_async_copy(attended.at[:, cols], attended_out.at[:, cols], o_sem.at[g])
 
     def wide(v):
         return v.astype(jnp.float32)
@@ -376,6 +385,7 @@
             before = near * on_c + beside * on_x + far * on_y
             prior[h] = (start + before).astype(jnp.bfloat16)
             final[h] = start + (wide(row) + far)
+        final_copy.start()
 
     top = rows // 2
 
@@ -407,15 +417,16 @@
                 attended[first : first + top, h * size : (h + 1) * size] = (
                     raw * scale * gain
                 ).astype(jnp.bfloat16)
+        slab_copy(g).start()
 
     steps = hops * PARTS
 
     squares[...] = jnp.zeros_like(squares)
     convert(z)
 
-    @pl.loop(0, chunks)
+    @pl.loop(0, early)
     def _(i):
-        @pl.when(i + AHEAD < chunks)
+        @pl.when(i + AHEAD <= early)
         def _():
             send_own(i + AHEAD)
 
@@ -463,21 +474,38 @@
             def _():
                 finish(now)
 
-        @pl.when(i == early + LAG)
-        def _():
-            state_one()
-
+    send_own(early + 1)
+    pass_near(early)
+    for ch in range(early - LAG, early):
+        pass_far(ch)
+
+    @pl.loop(early - LAG - 1, early)
+    def _(ch):
+        project(ch)
+
+    state_one()
     state_two()
-    pass_far(chunks - 2)
-    state_three()
-    project(early + 1)
-    state_four()
-    pass_far(chunks - 1)
-    state_five()
-    for g in range(groups):
+    done = 0
+    for g in range(1, groups):
+        i = early + g
+        if i + 1 < chunks:
+            send_own(i + 1)
+        pass_near(i)
+        pass_far(i - 1)
+        project(i - 1)
+        if g == 1:
+            state_three()
+        if g == 2:
+            state_four()
+            state_five()
+        if i + 1 == chunks:
+            pass_far(i)
         if g >= 2:
-            project(early + g)
-        attend(g)
+            for k in range(done, g):
+                attend(k)
+            done = g
+    project(chunks - 1)
+    attend(groups - 1)
 
     @pl.loop(0, chunks)
     def _(ch):
@@ -498,6 +526,24 @@
 
     for copy in (to_sib, to_x, x_to_sib, to_y, y_to_sib):
         copy.wait_send()
+    for g in range(groups):
+        slab_copy(g).wait()
+    final_copy.wait()
+
+
+def settle(attended, final, attended_out, final_out, sems):
+    rows = attended.shape[0] // PARTS
+    heads = final.shape[0] // PARTS
+    copies = []
+    for p in range(PARTS):
+        at = pl.ds(p * rows, rows)
+        copies.append(pltpu.make_async_copy(attended.at[at], attended_out.at[at], sems.at[0, p]))
+        at = pl.ds(p * heads, heads)
+        copies.append(pltpu.make_async_copy(final.at[at], final_out.at[at], sems.at[1, p]))
+    for copy in copies:
+        copy.start()
+    for copy in copies:
+        copy.wait()
 
 
 def fused(depth_z, tokens, norm_gain, w_query, w_key, w_value, out_gain, carried):
@@ -509,14 +555,15 @@
     any_spec = pl.BlockSpec(memory_space=pl.ANY)
     vmem_spec = pl.BlockSpec(memory_space=pltpu.VMEM)
     dma = pltpu.SemaphoreType.DMA
-    return pl.pallas_call(
+    shapes = (
+        jax.ShapeDtypeStruct((rows, width), jnp.bfloat16),
+        jax.ShapeDtypeStruct(carried.shape, jnp.float32),
+    )
+    results = pl.pallas_call(
         functools.partial(kernel, depth_z),
-        out_shape=(
-            jax.ShapeDtypeStruct((rows, width), jnp.bfloat16),
-            jax.ShapeDtypeStruct(carried.shape, jnp.float32),
-        ),
+        out_shape=shapes,
         in_specs=[any_spec, vmem_spec, any_spec, any_spec, any_spec, vmem_spec, vmem_spec],
-        out_specs=(vmem_spec, vmem_spec),
+        out_specs=(any_spec, any_spec),
         scratch_shapes=[
             pltpu.VMEM((depth_z, rows, shard), jnp.bfloat16),
             pltpu.VMEM((depth_z, rows, shard), jnp.bfloat16),
@@ -537,6 +584,9 @@
             dma((2, depth_z, PARTS)),
             dma((5,)),
             dma((5,)),
+            pltpu.VMEM((rows, width), jnp.bfloat16),
+            pltpu.VMEM(carried.shape, jnp.float32),
+            dma((width // GROUP + 1,)),
         ],
         compiler_params=pltpu.CompilerParams(
             collective_id=0, has_side_effects=True, vmem_limit_bytes=56 * 1024 * 1024
@@ -545,6 +595,13 @@
             flops=6 * rows * features * width, bytes_accessed=8 * depth * width, transcendentals=0
         ),
     )(tokens, norm_gain.reshape(depth_z, 1, shard), w_query, w_key, w_value, out_gain[None], carried)
+    return pl.pallas_call(
+        settle,
+        out_shape=shapes,
+        in_specs=[any_spec, any_spec],
+        out_specs=(any_spec, any_spec),
+        scratch_shapes=[dma((2, PARTS))],
+    )(*results)
 
 
 def solution(mesh):

time: 131 us -> 169 us (1.29)
  Pallas kernels: 126 us -> 168 us
  local copies, waits for them, and re-layouts: 3.12 us -> 0 us
    pallas_call x1 -> x2, Pallas kernels: 126 us -> 168 us  [the longest x1 119 us: fused(): pl.pallas_call(functools.partial(kernel, depth_z), out_shape=shapes, in_s...]
    unnamed x4 -> x0, local copies, waits for them, and re-layouts: 3.12 us -> none
where the time goes in v3:
time: 169 us
  Pallas kernels  168 us (99%)
    pallas_call x1, Pallas kernels, fused(): pl.pallas_call(functools.partial(kernel, depth_z), out_shape=shapes, in_s...  119 us
    pallas_call x1, Pallas kernels, fused(): pl.pallas_call(settle, out_shape=shapes, in_specs=[any_spec, any_spec], o...  48.8 us

profile of v3, /device:TPU:0, one launch (start us, length us, event | category | flops | bytes accessed | tf_op | source)
XLA Modules:
  0.0 168.9 jit_solution(12395792383129550197)
XLA Ops:
  0.6 119.4 %shard_map.86 = (bf16[512,1024]{1,0:T(8,128)(2,1)}, f32[8,128,128]{2,1,0:T(8,128)}) custom-call(bf16[512,1024]{1,0:T(8,128)(2,1)} %tokens.1, f32[4,1,1024]{2,1,0:T(1,128)} %bitcast.2, bf16[512,1024]{1,0:T(8,128)(2,1)} %w_query.1, bf16[512,1024]{1,0:T(8,128)(2,1)} %w_key.1, bf16[512,1024]{1,0:T(8,128)(2,1)} %w_value.1, f32[1,1024]{1,0:T(1,128)} %bitcast.3, ...), custom_call_target="tpu_custom_call" | custom-call | flops 12884901888 | bytes 4194304 | tf_op jit(solution)/shard_map/pallas_call | solution.py:562
  120.1 48.8 %shard_map.87 = (bf16[512,1024]{1,0:T(8,128)(2,1)}, f32[8,128,128]{2,1,0:T(8,128)}) custom-call(bf16[512,1024]{1,0:T(8,128)(2,1)} %get-tuple-element.4.attended, f32[8,128,128]{2,1,0:T(8,128)} %get-tuple-element.5.final), custom_call_target="tpu_custom_call" | custom-call | tf_op jit(solution)/shard_map/pallas_call | solution.py:598

commit v4 on v3

--- a/solution.py
+++ b/solution.py
@@ -12,7 +12,7 @@
 GROUP = 256
 PARTS = 4
 AHEAD = 2
-LAG = 2
+LAG = 1
 LANES = 128
 
 
@@ -426,11 +426,8 @@
 
     @pl.loop(0, early)
     def _(i):
-        @pl.when(i + AHEAD <= early)
-        def _():
-            send_own(i + AHEAD)
-
         pass_near(i)
+        send_own(i + AHEAD)
 
         @pl.when(i >= LAG)
         def _():
@@ -474,10 +471,8 @@
             def _():
                 finish(now)
 
-    send_own(early + 1)
     pass_near(early)
-    for ch in range(early - LAG, early):
-        pass_far(ch)
+    pass_far(early - 1)
 
     @pl.loop(early - LAG - 1, early)
     def _(ch):
@@ -485,26 +480,35 @@
 
     state_one()
     state_two()
-    done = 0
-    for g in range(1, groups):
+    send_own(early + 2)
+    for g in range(1, groups - 1):
         i = early + g
-        if i + 1 < chunks:
-            send_own(i + 1)
         pass_near(i)
         pass_far(i - 1)
-        project(i - 1)
         if g == 1:
             state_three()
-        if g == 2:
+        if g == groups - 2:
             state_four()
-            state_five()
-        if i + 1 == chunks:
-            pass_far(i)
-        if g >= 2:
-            for k in range(done, g):
-                attend(k)
-            done = g
-    project(chunks - 1)
+        if i + AHEAD < chunks:
+            send_own(i + AHEAD)
+        project(i - 1)
+    state_five()
+    for g in range(groups - 2):
+        attend(g)
+
+    last = chunks - 1
+    pass_near(last)
+    acc[last] = jnp.zeros((rows, GROUP), jnp.float32)
+    for kind, owner in ((2, seq), (5, xn), (6, yn)):
+        incoming(last, kind).wait_recv()
+        accumulate(last, owner // 2)
+    pass_far(last - 1)
+    project(last - 1)
+    pass_far(last)
+    attend(groups - 2)
+    incoming(last, 7).wait_recv()
+    accumulate(last, diag // 2)
+    finish(last)
     attend(groups - 1)
 
     @pl.loop(0, chunks)
@@ -531,19 +535,25 @@
     final_copy.wait()
 
 
-def settle(attended, final, attended_out, final_out, sems):
+def settle(attended, final, attended_out, final_out, held, held_final, sem_in, sem_out):
     rows = attended.shape[0] // PARTS
     heads = final.shape[0] // PARTS
-    copies = []
+    comes, goes = [], []
     for p in range(PARTS):
-        at = pl.ds(p * rows, rows)
-        copies.append(pltpu.make_async_copy(attended.at[at], attended_out.at[at], sems.at[0, p]))
-        at = pl.ds(p * heads, heads)
-        copies.append(pltpu.make_async_copy(final.at[at], final_out.at[at], sems.at[1, p]))
-    for copy in copies:
+        for k, count, source, here, target in (
+            (0, rows, attended, held, attended_out),
+            (1, heads, final, held_final, final_out),
+        ):
+            at = pl.ds(p * count, count)
+            comes.append(pltpu.make_async_copy(source.at[at], here.at[at], sem_in.at[k, p]))
+            goes.append(pltpu.make_async_copy(here.at[at], target.at[at], sem_out.at[k, p]))
+    for copy in comes:
         copy.start()
-    for copy in copies:
+    for copy, onward in zip(comes, goes):
         copy.wait()
+        onward.start()
+    for onward in goes:
+        onward.wait()
 
 
 def fused(depth_z, tokens, norm_gain, w_query, w_key, w_value, out_gain, carried):
@@ -600,12 +610,18 @@
         out_shape=shapes,
         in_specs=[any_spec, any_spec],
         out_specs=(any_spec, any_spec),
-        scratch_shapes=[dma((2, PARTS))],
+        scratch_shapes=[
+            pltpu.VMEM((rows, width), jnp.bfloat16),
+            pltpu.VMEM(carried.shape, jnp.float32),
+            dma((2, PARTS)),
+            dma((2, PARTS)),
+        ],
+        compiler_params=pltpu.CompilerParams(vmem_limit_bytes=60 * 1024 * 1024),
     )(*results)
 
 
 def solution(mesh):
-    square = mesh.shape["seq"] == 8
+    square = mesh.shape["seq"] == 8 and mesh.shape["tensor"] == 4
 
     def local(tokens, *rest):
         if square and tokens.shape[0] == BLOCK:

time: 169 us -> 120 us (0.71)
  Pallas kernels: 168 us -> 119 us
    pallas_call x1, Pallas kernels: 48.8 us -> 2.23 us  [fused(): pl.pallas_call(settle, out_shape=shapes, in_specs=[any_spec, any_spec], o...]
    pallas_call x1, Pallas kernels: 119 us -> 117 us  [fused(): pl.pallas_call(functools.partial(kernel, depth_z), out_shape=shapes, in_s...]
where the time goes in v4:
time: 120 us
  Pallas kernels  119 us (99%)
    pallas_call x1, Pallas kernels, fused(): pl.pallas_call(functools.partial(kernel, depth_z), out_shape=shapes, in_s...  117 us

profile of v4, /device:TPU:0, one launch (start us, length us, event | category | flops | bytes accessed | tf_op | source)
XLA Modules:
  0.0 119.9 jit_solution(17162655941550670410)
XLA Ops:
  0.6 117.0 %shard_map.86 = (bf16[512,1024]{1,0:T(8,128)(2,1)}, f32[8,128,128]{2,1,0:T(8,128)}) custom-call(bf16[512,1024]{1,0:T(8,128)(2,1)} %tokens.1, f32[4,1,1024]{2,1,0:T(1,128)} %bitcast.2, bf16[512,1024]{1,0:T(8,128)(2,1)} %w_query.1, bf16[512,1024]{1,0:T(8,128)(2,1)} %w_key.1, bf16[512,1024]{1,0:T(8,128)(2,1)} %w_value.1, f32[1,1024]{1,0:T(1,128)} %bitcast.3, ...), custom_call_target="tpu_custom_call" | custom-call | flops 12884901888 | bytes 4194304 | tf_op jit(solution)/shard_map/pallas_call | solution.py:572
  117.7 2.2 %shard_map.87 = (bf16[512,1024]{1,0:T(8,128)(2,1)}, f32[8,128,128]{2,1,0:T(8,128)}) custom-call(bf16[512,1024]{1,0:T(8,128)(2,1)} %get-tuple-element.4.attended, f32[8,128,128]{2,1,0:T(8,128)} %get-tuple-element.5.final), custom_call_target="tpu_custom_call" | custom-call | tf_op jit(solution)/shard_map/pallas_call | solution.py:608

commit v5 on v4

--- a/solution.py
+++ b/solution.py
@@ -11,8 +11,8 @@
 MESH = pl.DeviceIdType.MESH
 GROUP = 256
 PARTS = 4
-AHEAD = 2
-LAG = 1
+AHEAD = 3
+LAG = 2
 LANES = 128
 
 
@@ -427,7 +427,14 @@
     @pl.loop(0, early)
     def _(i):
         pass_near(i)
-        send_own(i + AHEAD)
+
+        @pl.when(i + AHEAD <= early)
+        def _():
+            send_own(i + AHEAD)
+
+        @pl.when(i == early - 1)
+        def _():
+            send_own(early + 1)
 
         @pl.when(i >= LAG)
         def _():
@@ -472,9 +479,11 @@
                 finish(now)
 
     pass_near(early)
+    pass_far(early - 2)
+    project(early - 3)
     pass_far(early - 1)
 
-    @pl.loop(early - LAG - 1, early)
+    @pl.loop(early - 2, early)
     def _(ch):
         project(ch)
 
@@ -489,8 +498,8 @@
             state_three()
         if g == groups - 2:
             state_four()
-        if i + AHEAD < chunks:
-            send_own(i + AHEAD)
+        if i + 2 < chunks:
+            send_own(i + 2)
         project(i - 1)
     state_five()
     for g in range(groups - 2):

time: 120 us -> 121 us (level)
  no operation moved by 1% of the time
where the time goes in v5:
time: 121 us
  Pallas kernels  120 us (99%)
    pallas_call x1, Pallas kernels, fused(): pl.pallas_call(functools.partial(kernel, depth_z), out_shape=shapes, in_s...  118 us

profile of v5, /device:TPU:0, one launch (start us, length us, event | category | flops | bytes accessed | tf_op | source)
XLA Modules:
  0.0 120.8 jit_solution(9378049469976159573)
XLA Ops:
  0.6 117.9 %shard_map.86 = (bf16[512,1024]{1,0:T(8,128)(2,1)}, f32[8,128,128]{2,1,0:T(8,128)}) custom-call(bf16[512,1024]{1,0:T(8,128)(2,1)} %tokens.1, f32[4,1,1024]{2,1,0:T(1,128)} %bitcast.2, bf16[512,1024]{1,0:T(8,128)(2,1)} %w_query.1, bf16[512,1024]{1,0:T(8,128)(2,1)} %w_key.1, bf16[512,1024]{1,0:T(8,128)(2,1)} %w_value.1, f32[1,1024]{1,0:T(1,128)} %bitcast.3, ...), custom_call_target="tpu_custom_call" | custom-call | flops 12884901888 | bytes 4194304 | tf_op jit(solution)/shard_map/pallas_call | solution.py:581
  118.5 2.2 %shard_map.87 = (bf16[512,1024]{1,0:T(8,128)(2,1)}, f32[8,128,128]{2,1,0:T(8,128)}) custom-call(bf16[512,1024]{1,0:T(8,128)(2,1)} %get-tuple-element.4.attended, f32[8,128,128]{2,1,0:T(8,128)} %get-tuple-element.5.final), custom_call_target="tpu_custom_call" | custom-call | tf_op jit(solution)/shard_map/pallas_call | solution.py:617

commit v6 on v4

--- a/solution.py
+++ b/solution.py
@@ -86,8 +86,8 @@
     w_value,
     out_gain,
     carried,
-    attended_out,
-    final_out,
+    attended,
+    final,
     tok,
     scaled,
     squares,
@@ -107,9 +107,6 @@
     t_recv,
     s_send,
     s_recv,
-    attended,
-    final,
-    o_sem,
 ):
     rows, shard = tokens.shape
     depth = w_query.shape[0]
@@ -341,12 +338,6 @@
     y_to_sib = state_copy(4, sum_in.at[1, mine], sum_in.at[1, mine], sib)
     x_from_sib = state_copy(2, sum_in.at[0, theirs], sum_in.at[0, theirs], sib)
     y_from_sib = state_copy(4, sum_in.at[1, theirs], sum_in.at[1, theirs], sib)
-
-    final_copy = pltpu.make_async_copy(final, final_out, o_sem.at[groups])
-
-    def slab_copy(g):
-        cols = pl.ds(g * GROUP, GROUP)
-        return pltpu.make_async_copy(attended.at[:, cols], attended_out.at[:, cols], o_sem.at[g])
 
     def wide(v):
         return v.astype(jnp.float32)
@@ -385,7 +376,6 @@
             before = near * on_c + beside * on_x + far * on_y
             prior[h] = (start + before).astype(jnp.bfloat16)
             final[h] = start + (wide(row) + far)
-        final_copy.start()
 
     top = rows // 2
 
@@ -417,7 +407,6 @@
                 attended[first : first + top, h * size : (h + 1) * size] = (
                     raw * scale * gain
                 ).astype(jnp.bfloat16)
-        slab_copy(g).start()
 
     steps = hops * PARTS
 
@@ -530,30 +519,21 @@
 
     for copy in (to_sib, to_x, x_to_sib, to_y, y_to_sib):
         copy.wait_send()
-    for g in range(groups):
-        slab_copy(g).wait()
-    final_copy.wait()
-
-
-def settle(attended, final, attended_out, final_out, held, held_final, sem_in, sem_out):
+
+
+def settle(attended, final, attended_out, final_out, sems):
     rows = attended.shape[0] // PARTS
     heads = final.shape[0] // PARTS
-    comes, goes = [], []
+    copies = []
     for p in range(PARTS):
-        for k, count, source, here, target in (
-            (0, rows, attended, held, attended_out),
-            (1, heads, final, held_final, final_out),
-        ):
-            at = pl.ds(p * count, count)
-            comes.append(pltpu.make_async_copy(source.at[at], here.at[at], sem_in.at[k, p]))
-            goes.append(pltpu.make_async_copy(here.at[at], target.at[at], sem_out.at[k, p]))
-    for copy in comes:
+        at = pl.ds(p * rows, rows)
+        copies.append(pltpu.make_async_copy(attended.at[at], attended_out.at[at], sems.at[0, p]))
+        at = pl.ds(p * heads, heads)
+        copies.append(pltpu.make_async_copy(final.at[at], final_out.at[at], sems.at[1, p]))
+    for copy in copies:
         copy.start()
-    for copy, onward in zip(comes, goes):
+    for copy in copies:
         copy.wait()
-        onward.start()
-    for onward in goes:
-        onward.wait()
 
 
 def fused(depth_z, tokens, norm_gain, w_query, w_key, w_value, out_gain, carried):
@@ -571,9 +551,9 @@
     )
     results = pl.pallas_call(
         functools.partial(kernel, depth_z),
-        out_shape=shapes,
+        out_shape=tuple(pltpu.VMEM(s.shape, s.dtype) for s in shapes),
         in_specs=[any_spec, vmem_spec, any_spec, any_spec, any_spec, vmem_spec, vmem_spec],
-        out_specs=(any_spec, any_spec),
+        out_specs=(vmem_spec, vmem_spec),
         scratch_shapes=[
             pltpu.VMEM((depth_z, rows, shard), jnp.bfloat16),
             pltpu.VMEM((depth_z, rows, shard), jnp.bfloat16),
@@ -594,9 +574,6 @@
             dma((2, depth_z, PARTS)),
             dma((5,)),
             dma((5,)),
-            pltpu.VMEM((rows, width), jnp.bfloat16),
-            pltpu.VMEM(carried.shape, jnp.float32),
-            dma((width // GROUP + 1,)),
         ],
         compiler_params=pltpu.CompilerParams(
             collective_id=0, has_side_effects=True, vmem_limit_bytes=56 * 1024 * 1024
@@ -610,13 +587,7 @@
         out_shape=shapes,
         in_specs=[any_spec, any_spec],
         out_specs=(any_spec, any_spec),
-        scratch_shapes=[
-            pltpu.VMEM((rows, width), jnp.bfloat16),
-            pltpu.VMEM(carried.shape, jnp.float32),
-            dma((2, PARTS)),
-            dma((2, PARTS)),
-        ],
-        compiler_params=pltpu.CompilerParams(vmem_limit_bytes=60 * 1024 * 1024),
+        scratch_shapes=[dma((2, PARTS))],
     )(*results)
 
 

time: 120 us -> 168 us (1.40)
  Pallas kernels: 119 us -> 165 us
  local copies, waits for them, and re-layouts: 0 us -> 1.76 us
    pallas_call x1, Pallas kernels: 2.23 us -> 48.8 us  [fused(): pl.pallas_call(settle, out_shape=shapes, in_specs=[any_spec, any_spec], o...]
    unnamed x0 -> x4, local copies, waits for them, and re-layouts: none -> 1.76 us
where the time goes in v6:
time: 168 us
  Pallas kernels  165 us (98%)
  local copies, waits for them, and re-layouts  1.76 us (1%)
    pallas_call x1, Pallas kernels, fused(): pl.pallas_call(functools.partial(kernel, depth_z), out_shape=tuple((pltpu...  117 us
    pallas_call x1, Pallas kernels, fused(): pl.pallas_call(settle, out_shape=shapes, in_specs=[any_spec, any_spec], o...  48.8 us

profile of v6, /device:TPU:0, one launch (start us, length us, event | category | flops | bytes accessed | tf_op | source)
XLA Modules:
  0.0 167.9 jit_solution(3230426308205152080)
XLA Ops:
  0.6 116.6 %shard_map.86 = (bf16[512,1024]{1,0:T(8,128)(2,1)S(1)}, f32[8,128,128]{2,1,0:T(8,128)S(1)}) custom-call(bf16[512,1024]{1,0:T(8,128)(2,1)} %tokens.1, f32[4,1,1024]{2,1,0:T(1,128)} %bitcast.2, bf16[512,1024]{1,0:T(8,128)(2,1)} %w_query.1, bf16[512,1024]{1,0:T(8,128)(2,1)} %w_key.1, bf16[512,1024]{1,0:T(8,128)(2,1)} %w_value.1, f32[1,1024]{1,0:T(1,128)} %bitcast.3, ...), custom_call_target="tpu_custom_call" | custom-call | flops 12884901888 | bytes 4194304 | tf_op jit(solution)/shard_map/pallas_call | solution.py:552
  117.3 0.0 copy-start
  117.3 1.0 copy-done
  118.3 0.0 copy-start.1
  118.3 0.8 copy-done.1
  119.1 48.8 %shard_map.87 = (bf16[512,1024]{1,0:T(8,128)(2,1)}, f32[8,128,128]{2,1,0:T(8,128)}) custom-call(bf16[512,1024]{1,0:T(8,128)(2,1)} %copy-done, f32[8,128,128]{2,1,0:T(8,128)} %copy-done.1), custom_call_target="tpu_custom_call" | custom-call | tf_op jit(solution)/shard_map/pallas_call | solution.py:585
Async XLA Ops:
  117.3 1.0 copy-start
  118.3 0.8 copy-start.1

commit v7 on v6

--- a/solution.py
+++ b/solution.py
@@ -521,21 +521,6 @@
         copy.wait_send()
 
 
-def settle(attended, final, attended_out, final_out, sems):
-    rows = attended.shape[0] // PARTS
-    heads = final.shape[0] // PARTS
-    copies = []
-    for p in range(PARTS):
-        at = pl.ds(p * rows, rows)
-        copies.append(pltpu.make_async_copy(attended.at[at], attended_out.at[at], sems.at[0, p]))
-        at = pl.ds(p * heads, heads)
-        copies.append(pltpu.make_async_copy(final.at[at], final_out.at[at], sems.at[1, p]))
-    for copy in copies:
-        copy.start()
-    for copy in copies:
-        copy.wait()
-
-
 def fused(depth_z, tokens, norm_gain, w_query, w_key, w_value, out_gain, carried):
     rows, shard = tokens.shape
     depth, width = w_query.shape
@@ -549,7 +534,7 @@
         jax.ShapeDtypeStruct((rows, width), jnp.bfloat16),
         jax.ShapeDtypeStruct(carried.shape, jnp.float32),
     )
-    results = pl.pallas_call(
+    return pl.pallas_call(
         functools.partial(kernel, depth_z),
         out_shape=tuple(pltpu.VMEM(s.shape, s.dtype) for s in shapes),
         in_specs=[any_spec, vmem_spec, any_spec, any_spec, any_spec, vmem_spec, vmem_spec],
@@ -582,13 +567,6 @@
             flops=6 * rows * features * width, bytes_accessed=8 * depth * width, transcendentals=0
         ),
     )(tokens, norm_gain.reshape(depth_z, 1, shard), w_query, w_key, w_value, out_gain[None], carried)
-    return pl.pallas_call(
-        settle,
-        out_shape=shapes,
-        in_specs=[any_spec, any_spec],
-        out_specs=(any_spec, any_spec),
-        scratch_shapes=[dma((2, PARTS))],
-    )(*results)
 
 
 def solution(mesh):

time: 168 us -> 119 us (0.71)
  Pallas kernels: 165 us -> 117 us
    pallas_call x1 -> x0, Pallas kernels: 48.8 us -> none  [fused(): pl.pallas_call(settle, out_shape=shapes, in_specs=[any_spec, any_spec], o...]
where the time goes in v7:
time: 119 us
  Pallas kernels  117 us (98%)
  local copies, waits for them, and re-layouts  1.77 us (1%)
    pallas_call x1, Pallas kernels, fused(): pl.pallas_call(functools.partial(kernel, depth_z), out_shape=tuple((pltpu...  117 us

profile of v7, /device:TPU:0, one launch (start us, length us, event | category | flops | bytes accessed | tf_op | source)
XLA Modules:
  0.0 119.0 jit_solution(6728185156708772548)
XLA Ops:
  0.6 116.6 %shard_map.86 = (bf16[512,1024]{1,0:T(8,128)(2,1)S(1)}, f32[8,128,128]{2,1,0:T(8,128)S(1)}) custom-call(bf16[512,1024]{1,0:T(8,128)(2,1)} %tokens.1, f32[4,1,1024]{2,1,0:T(1,128)} %bitcast.2, bf16[512,1024]{1,0:T(8,128)(2,1)} %w_query.1, bf16[512,1024]{1,0:T(8,128)(2,1)} %w_key.1, bf16[512,1024]{1,0:T(8,128)(2,1)} %w_value.1, f32[1,1024]{1,0:T(1,128)} %bitcast.3, ...), custom_call_target="tpu_custom_call" | custom-call | flops 12884901888 | bytes 4194304 | tf_op jit(solution)/shard_map/pallas_call | solution.py:537
  117.3 1.0 copy.11
  118.3 0.8 copy.12
